TPU v7x, 512 devices: a whole 4x4x16 slice. The times are simulated.
512 devices in a mesh: dp: 16 (over y, x), expert: 32 (over z, core).
Axes of the slice: x: 4, y: 4, z: 16, core: 2. Of those that a mesh axis runs over, the one named last changes fastest.
Arguments:
- out_grad: bfloat16 [131072, 2048], P(('dp', 'expert')), may hold values from -6 to 6
- hidden_act: bfloat16 [131072, 2, 768], P(('dp', 'expert')), may hold values from -4 to 4
- expert_ids: int32 [131072, 2], P(('dp', 'expert')), may hold values from 0 to 31, all different within a row; in each aligned block of 256 rows (0 to 255, 256 to 511, ...) at most 32 rows name the same one
- gate_weight: bfloat16 [131072, 2], P(('dp', 'expert')), may hold values from 0.049804688 to 1
- down_weight: bfloat16 [32, 768, 2048], P('expert', 'dp'), may hold values from -0.21875 to 0.21875
- first_moment: float32 [32, 768, 2048], P('expert', 'dp'), may hold values from -12 to 12
- second_moment: float32 [32, 768, 2048], P('expert', 'dp'), may hold values from 0.5 to 8
Outputs:
- hidden_grad: bfloat16 [131072, 2, 768], P(('dp', 'expert'))
- gate_grad: float32 [131072, 2], P(('dp', 'expert'))
- moment_new: float32 [32, 768, 2048], P('expert', 'dp')
- second_new: float32 [32, 768, 2048], P('expert', 'dp')
- update: float32 [32, 768, 2048], P('expert', 'dp')
Inputs may be any that keep to these rules, and one draw needn't show every extreme that they name: `expert_ids`: A token's 2 ids differ. Among the slots of one device's 256 tokens, no expert is named more than 32 times, and in every draw some expert is named exactly 32 times by one device's slots.
All inputs are finite; a program needn't handle non-finite values.
Results may differ from a plain program's by a relative error of at most 0.013.
Values may be sent and summed in bfloat16 or wider, within the bound.
A program may use at most 64 MiB of HBM per device.

v0:
```python
import jax
import jax.numpy as jnp
from jax import lax
from jax.sharding import PartitionSpec as P

STEP = 11


beta_one = 0.9
beta_two = 0.999
adam_eps = 1e-08


def slot_positions(flat_ids, experts):
    onehot = (flat_ids[:, None] == jnp.arange(experts, dtype=jnp.int32)[None, :]).astype(jnp.int32)
    running = jnp.cumsum(onehot, axis=0, dtype=jnp.int32)
    return jnp.sum(running * onehot, axis=1, dtype=jnp.int32) - 1


def reply_rows(received_grad, full_weight):
    product = lax.dot_general(
        received_grad, full_weight, (((2,), (1,)), ((), ())), preferred_element_type=jnp.float32
    )
    return product.astype(jnp.bfloat16)


def body(out_grad, hidden_act, expert_ids, gate_weight, down_weight, first_moment, second_moment):
    tok_rows, top_count = expert_ids.shape
    model_width = out_grad.shape[1]
    hidden = hidden_act.shape[2]
    n_expert = lax.axis_size("expert")
    capacity = 2 * tok_rows * top_count // n_expert
    slot_total = n_expert * capacity
    slot_count = tok_rows * top_count
    flat_ids = expert_ids.reshape(-1)
    position = slot_positions(flat_ids, n_expert)
    target = flat_ids * capacity + position
    matches = target[:, None] == jnp.arange(slot_total, dtype=jnp.int32)[None, :]
    filled = jnp.any(matches, axis=0)
    source = jnp.sum(
        jnp.where(matches, jnp.arange(slot_count, dtype=jnp.int32)[:, None], 0),
        axis=0,
        dtype=jnp.int32,
    )
    source_token = source // top_count
    zero_bf = jnp.zeros((), jnp.bfloat16)
    send_grad = jnp.where(
        filled[:, None], jnp.take(out_grad, source_token, axis=0), zero_bf
    ).reshape(n_expert, capacity, model_width)
    send_act = jnp.where(
        filled[:, None], jnp.take(hidden_act.reshape(-1, hidden), source, axis=0), zero_bf
    ).reshape(n_expert, capacity, hidden)
    send_gate = jnp.where(
        filled, jnp.take(gate_weight.reshape(-1), source, axis=0), zero_bf
    ).reshape(n_expert, capacity)
    full_weight = lax.all_gather(down_weight[0], "dp", axis=0, tiled=True)
    grads_in, acts_in, gates_in = (
        lax.all_to_all(send_grad, "expert", split_axis=0, concat_axis=0, tiled=True),
        lax.all_to_all(send_act, "expert", split_axis=0, concat_axis=0, tiled=True),
        lax.all_to_all(send_gate, "expert", split_axis=0, concat_axis=0, tiled=True),
    )
    returned = lax.all_to_all(
        reply_rows(grads_in, full_weight), "expert", split_axis=0, concat_axis=0, tiled=True
    )
    acts_flat = acts_in.reshape(slot_total, hidden)
    scaled = (
        gates_in.reshape(slot_total, 1).astype(jnp.float32)
        * grads_in.reshape(slot_total, model_width).astype(jnp.float32)
    ).astype(jnp.bfloat16)
    gradient = lax.psum_scatter(
        lax.dot_general(
            acts_flat, scaled, (((0,), (0,)), ((), ())), preferred_element_type=jnp.float32
        ).astype(jnp.bfloat16),
        "dp",
        scatter_dimension=0,
        tiled=True,
    ).astype(jnp.float32)
    moment_new = beta_one * first_moment[0] + (1.0 - beta_one) * gradient
    second_new = beta_two * second_moment[0] + (1.0 - beta_two) * gradient * gradient
    fix_one = 1.0 - beta_one**STEP
    fix_two = 1.0 - beta_two**STEP
    update = moment_new / fix_one / (jnp.sqrt(second_new / fix_two) + adam_eps)
    dh_slot = jnp.take(returned.reshape(slot_total, hidden), target, axis=0)
    hidden_grad = (
        (gate_weight.reshape(-1, 1).astype(jnp.float32) * dh_slot.astype(jnp.float32))
        .astype(jnp.bfloat16)
        .reshape(tok_rows, top_count, hidden)
    )
    gate_grad = jnp.sum(
        hidden_act.reshape(-1, hidden).astype(jnp.float32) * dh_slot.astype(jnp.float32), axis=1
    ).reshape(tok_rows, top_count)
    return (hidden_grad, gate_grad, moment_new[None], second_new[None], update[None])


def solution(mesh):
    return jax.shard_map(
        body,
        mesh=mesh,
        in_specs=(
            P(("dp", "expert"), None),
            P(("dp", "expert"), None, None),
            P(("dp", "expert"), None),
            P(("dp", "expert"), None),
            P("expert", "dp", None),
            P("expert", "dp", None),
            P("expert", "dp", None),
        ),
        out_specs=(
            P(("dp", "expert"), None, None),
            P(("dp", "expert"), None),
            P("expert", "dp", None),
            P("expert", "dp", None),
            P("expert", "dp", None),
        ),
        check_vma=False,
    )
```

profile of v0, /device:TPU:6, one launch (start us, length us, event | category | flops | bytes accessed | tf_op | source)
XLA Modules:
  0.0 443.6 jit_solution(1147790714129969665)
XLA Ops:
  7.2 0.9 copy.44
  8.1 0.1 reshape.302
  8.2 0.1 eq.39
  8.4 1.2 reduce-window.6
  9.6 0.2 slice_reduce_fusion
  9.8 0.1 fusion.15
  9.9 0.3 select_reduce_fusion
  10.2 0.4 fusion.4
  10.6 0.1 reduce_sum.38
  10.7 0.1 reduce_or.12
  10.8 0.8 copy.50
  11.6 0.2 reshape.306
  11.8 6.8 %gather_fusion.3 = bf16[1024]{0:T(1024)(128)(2,1)S(1)} fusion(bf16[512]{0:T(512)(128)(2,1)S(1)} %reshape.306, s32[1024]{0:T(1024)S(1)} %broadcast_clamp_fusion), kind=kCustom, calls=%fused_computation.3 | custom fusion | bytes 8192 | tf_op jit(solution)/shard_map/jit(_take)/gather | solution.py:54
  18.6 0.1 gather.31
  18.7 0.6 copy.51
  19.3 15.5 %all-to-all-start.3 = ((bf16[32,1,32]{2,1,0:T(2,128)(2,1)}), bf16[32,1,32]{2,1,0:T(2,128)(2,1)S(1)}, u32[]{:S(2)}, u32[]{:S(2)}) async-start(bf16[32,1,32]{2,1,0:T(2,128)(2,1)} %copy.51), calls=%async_computation.3 | async-start | bytes 32768 | tf_op jit(solution)/shard_map/all_to_all | solution.py:60
  34.9 0.1 broadcast_in_dim.94
  35.0 6.0 %gather_fusion = bf16[1024,2048]{1,0:T(8,128)(2,1)} fusion(bf16[256,2048]{1,0:T(8,128)(2,1)S(1)} %copy-done, s32[1024]{0:T(1024)S(1)} %broadcast_clamp_fusion.1), kind=kCustom, calls=%fused_computation | custom fusion | bytes 8392704 | tf_op jit(solution)/shard_map/jit(_take)/gather | solution.py:48
  41.0 3.9 select_select_fusion
  44.9 2.3 all-to-all-done.3
  47.2 10.1 %all-to-all-start = ((bf16[32,32,2048]{2,1,0:T(8,128)(2,1)}), bf16[32,32,2048]{2,1,0:T(8,128)(2,1)}, u32[]{:S(2)}, u32[]{:S(2)}) async-start(bf16[32,32,2048]{2,1,0:T(8,128)(2,1)} %select_select_fusion), calls=%async_computation | async-start | bytes 8388608 | tf_op jit(solution)/shard_map/all_to_all | solution.py:58
  57.4 0.7 all-gather.3.cloned.1.call-update
  58.1 0.3 reshape.305
  58.4 4.0 gather_fusion.2
  62.4 1.4 select_select_fusion.1
  63.8 177.0 %all-to-all-done = bf16[32,32,2048]{2,1,0:T(8,128)(2,1)} async-done(((bf16[32,32,2048]{2,1,0:T(8,128)(2,1)}), bf16[32,32,2048]{2,1,0:T(8,128)(2,1)}, u32[]{:S(2)}, u32[]{:S(2)}) %all-to-all-start) | async-done | bytes 4194336 | tf_op jit(solution)/shard_map/all_to_all | solution.py:58
  240.8 10.1 %all-to-all-start.2 = ((bf16[32,32,768]{2,1,0:T(8,128)(2,1)}), bf16[32,32,768]{2,1,0:T(8,128)(2,1)S(1)}, u32[]{:S(2)}, u32[]{:S(2)}) async-start(bf16[32,32,768]{2,1,0:T(8,128)(2,1)} %select_select_fusion.1), calls=%async_computation.2 | async-start | bytes 3145728 | tf_op jit(solution)/shard_map/all_to_all | solution.py:59
  251.0 7.8 %fusion.5 = bf16[32,32,768]{2,1,0:T(8,128)(2,1)} fusion(bf16[32,32,2048]{2,1,0:T(8,128)(2,1)} %all-to-all-done, bf16[1,768,2048]{2,1,0:T(8,128)(2,1)} %all-gather.3.cloned.1.call-done), kind=kOutput, calls=%fused_computation.16 | convolution fusion | flops 3222011904 | bytes 8912896 | tf_op jit(solution)/shard_map/dot_general | solution.py:21
  258.8 70.3 %all-to-all-done.2 = bf16[32,32,768]{2,1,0:T(8,128)(2,1)S(1)} async-done(((bf16[32,32,768]{2,1,0:T(8,128)(2,1)}), bf16[32,32,768]{2,1,0:T(8,128)(2,1)S(1)}, u32[]{:S(2)}, u32[]{:S(2)}) %all-to-all-start.2) | async-done | bytes 1572896 | tf_op jit(solution)/shard_map/all_to_all | solution.py:59
  329.1 1.2 copy-done.3
  330.3 4.0 all-to-all-start.1
  334.2 0.2 reduce-scatter.2.cloned.1.call-start
  334.5 8.0 %bitcast_convert_fusion = bf16[768,2048]{1,0:T(8,128)(2,1)} fusion(bf16[32,32,768]{2,1,0:T(8,128)(2,1)} %copy-done.3, bf16[32,32,2048]{2,1,0:T(8,128)(2,1)} %all-to-all-done, f32[32,32]{1,0:T(8,128)S(1)} %bitcast.59), kind=kOutput, calls=%fused_computation.5 | convolution fusion | flops 3229089792 | bytes 8916992 | tf_op jit(solution)/shard_map/dot_general | solution.py:71
  342.5 0.7 copy-done.6
  343.2 0.1 copy.43
  343.3 0.1 copy.49
  343.5 0.1 mul.90
  343.6 0.1 sub.17
  343.8 0.1 copy.47
  343.9 0.8 copy.48
  344.7 68.6 %all-to-all-done.1 = bf16[32,32,768]{2,1,0:T(8,128)(2,1)S(1)} async-done(((bf16[32,32,768]{2,1,0:T(8,128)(2,1)}), bf16[32,32,768]{2,1,0:T(8,128)(2,1)S(1)}, u32[]{:S(2)}, u32[]{:S(2)}) %all-to-all-start.1) | async-done | bytes 1572896 | tf_op jit(solution)/shard_map/all_to_all | solution.py:62
  413.2 2.0 gather_fusion.1
  415.3 0.3 gather.27
  415.6 0.8 copy-done.2
  416.4 3.9 fusion.9
  420.3 0.7 copy.52
  420.9 13.6 %reduce-scatter.2.cloned.1.call-done = bf16[48,2048]{1,0:T(8,128)(2,1)} async-done(((bf16[768,2048]{1,0:T(8,128)(2,1)}), bf16[48,2048]{1,0:T(8,128)(2,1)}) %reduce-scatter.2.cloned.1.call-update) | async-done | bytes 196624 | tf_op jit(solution)/shard_map/reduce_scatter | solution.py:70
  434.5 2.2 divide_bitcast_fusion
  (29 shorter events, 0.4 us)
Async XLA Ops:
  7.2 27.8 %copy-start = (bf16[256,2048]{1,0:T(8,128)(2,1)S(1)}, bf16[256,2048]{1,0:T(8,128)(2,1)}, u32[]{:S(2)}) copy-start(bf16[256,2048]{1,0:T(8,128)(2,1)} %param.7) | copy-start | bytes 3145732
  19.3 27.9 %all-to-all-start.3 = ((bf16[32,1,32]{2,1,0:T(2,128)(2,1)}), bf16[32,1,32]{2,1,0:T(2,128)(2,1)S(1)}, u32[]{:S(2)}, u32[]{:S(2)}) async-start(bf16[32,1,32]{2,1,0:T(2,128)(2,1)} %copy.51), calls=%async_computation.3 | async-start | bytes 32768 | tf_op jit(solution)/shard_map/all_to_all | solution.py:60
  44.9 13.2 %copy-start.1 = (bf16[256,2,768]{2,1,0:T(2,128)(2,1)S(1)}, bf16[256,2,768]{2,1,0:T(2,128)(2,1)}, u32[]{:S(2)}) copy-start(bf16[256,2,768]{2,1,0:T(2,128)(2,1)} %param.8) | copy-start | bytes 2359300
  47.2 193.6 %all-to-all-start = ((bf16[32,32,2048]{2,1,0:T(8,128)(2,1)}), bf16[32,32,2048]{2,1,0:T(8,128)(2,1)}, u32[]{:S(2)}, u32[]{:S(2)}) async-start(bf16[32,32,2048]{2,1,0:T(8,128)(2,1)} %select_select_fusion), calls=%async_computation | async-start | bytes 8388608 | tf_op jit(solution)/shard_map/all_to_all | solution.py:58
  57.3 193.6 %all-gather.3.cloned.1.call-start = ((), (), s32[]{:S(2)}) async-start(), calls=%async_computation.6 | async-start | bytes 3342336 | tf_op jit(solution)/shard_map/all_gather | solution.py:56
  240.8 88.3 %all-to-all-start.2 = ((bf16[32,32,768]{2,1,0:T(8,128)(2,1)}), bf16[32,32,768]{2,1,0:T(8,128)(2,1)S(1)}, u32[]{:S(2)}, u32[]{:S(2)}) async-start(bf16[32,32,768]{2,1,0:T(8,128)(2,1)} %select_select_fusion.1), calls=%async_computation.2 | async-start | bytes 3145728 | tf_op jit(solution)/shard_map/all_to_all | solution.py:59
  329.1 1.2 copy-start.3
  330.3 83.0 %all-to-all-start.1 = ((bf16[32,32,768]{2,1,0:T(8,128)(2,1)}), bf16[32,32,768]{2,1,0:T(8,128)(2,1)S(1)}, u32[]{:S(2)}, u32[]{:S(2)}) async-start(bf16[32,32,768]{2,1,0:T(8,128)(2,1)} %fusion.5), calls=%async_computation.1 | async-start | bytes 3145728 | tf_op jit(solution)/shard_map/all_to_all | solution.py:62
  334.2 100.3 %reduce-scatter.2.cloned.1.call-start = ((), (), s32[]{:S(2)}) async-start(), calls=%async_computation.5 | async-start | bytes 3342336 | tf_op jit(solution)/shard_map/reduce_scatter | solution.py:70
  342.5 0.7 copy-start.6
  342.5 0.8 copy-start.5
  415.2 1.1 copy-start.2
  416.4 18.1 %copy-start.4 = (f32[1,48,2048]{2,1,0:T(8,128)S(1)}, f32[1,48,2048]{2,1,0:T(8,128)}, u32[]{:S(2)}) copy-start(f32[1,48,2048]{2,1,0:T(8,128)} %param.12) | copy-start | bytes 1179652
Sparse Core Ops, SparseCore 0:
  61.2 63.5 all-gather.2
  342.7 91.8 reduce-scatter.1
where the time goes:
time: 444 us
  waiting for transfers between devices  333 us (75%)
  starting transfers between devices  39.9 us (9%)
  local copies, waits for them, and re-layouts  27.5 us (6%)
  matrix products  15.8 us (4%)
  between operations  14.3 us (3%)
  other arithmetic  13.5 us (3%)
    all_to_all x1, waiting for transfers between devices, body(): lax.all_to_all(send_grad, 'expert', split_axis=0, concat_axis=0, tiled=True)  177 us
    all_to_all x1, waiting for transfers between devices, body(): lax.all_to_all(send_act, 'expert', split_axis=0, concat_axis=0, tiled=True)  70.3 us
    all_to_all x1, waiting for transfers between devices, body(): lax.all_to_all(reply_rows(grads_in, full_weight), 'expert', split_axis=0,...  68.6 us
    all_to_all x1, starting transfers between devices, body(): lax.all_to_all(send_gate, 'expert', split_axis=0, concat_axis=0, tiled=True)  15.5 us
    reduce_scatter x1, waiting for transfers between devices, body(): lax.psum_scatter(lax.dot_general(acts_flat, scaled, (((0,), (0,)), ((), (...  13.6 us
    all_to_all x1, starting transfers between devices, body(): lax.all_to_all(send_grad, 'expert', split_axis=0, concat_axis=0, tiled=True)  10.1 us
    all_to_all x1, starting transfers between devices, body(): lax.all_to_all(send_act, 'expert', split_axis=0, concat_axis=0, tiled=True)  10.1 us
  transfers between devices with their start and end apart: 6, of which 5 were waited for; matrix products, arithmetic and copies ran while one was open for 9% of the time, Pallas kernels for 0%

commit v1 on v0

v1 whole, which is shorter than its diff:
```python
import functools

import jax
import jax.numpy as jnp
from jax import lax
from jax.experimental import pallas as pl
from jax.experimental.pallas import tpu as pltpu
from jax.sharding import PartitionSpec as P

STEP = 11
MESH = pl.DeviceIdType.MESH
BF = jnp.bfloat16
F32 = jnp.float32

beta_one = 0.9
beta_two = 0.999
adam_eps = 1e-08


def plane_kernel(
    sizes, grads_ref, hid_ref, ids_ref, gate_row_ref, gate_col_ref, w_ref, m_ref, v_ref,
    dh_ref, gg_ref, mo_ref, vo_ref, up_ref,
    s0, s1, send_a, send_g, recv_a, recv_at, recv_g, w_full, part, racc, reply, back,
    stage_r, stage_l, gfin, grecv,
    a_ss, a_rs, g_ss, g_rs, p_ss, p_rs, t_ss, t_rs, gr_ss, gr_rs, gl_ss, gl_rs,
    rr_ss, rr_rs, rl_ss, rl_rs, f_ss, f_rs,
):
    nz, nj, tok, cap, hid, nb, db = sizes
    half = nz // 2
    rows = hid // nz
    slots = nj * cap
    dp = lax.axis_index("dp")
    ez = lax.axis_index("expert")
    z = ez // 2
    core = lax.rem(ez, 2)
    j = dp * 2 + core
    z_up, z_down = lax.rem(z + 1, nz), lax.rem(z + nz - 1, nz)
    up, down, partner = (dp, z_up * 2 + core), (dp, z_down * 2 + core), (z, dp * 2 + core)
    crossed = dp != z

    def peer(i):
        t = lax.rem(j + i, nj)
        return t, (t // 2, z * 2 + lax.rem(t, 2))

    def chunk(t):
        return pl.ds(pl.multiple_of(t * cap, cap), cap)

    def shard(q):
        return pl.ds(pl.multiple_of(q * rows, rows), rows)

    barrier = pltpu.get_barrier_semaphore()

    @pl.loop(1, nj)
    def _(i):
        pl.semaphore_signal(barrier, inc=1, device_id=peer(i)[1], device_id_type=MESH)

    pl.semaphore_signal(barrier, inc=1, device_id=up, device_id_type=MESH)
    pl.semaphore_signal(barrier, inc=1, device_id=down, device_id_type=MESH)

    @pl.when(crossed)
    def _():
        pl.semaphore_signal(barrier, inc=1, device_id=partner, device_id_type=MESH)

    experts = lax.broadcasted_iota(jnp.int32, (nj, tok), 0)
    hot0 = (experts == ids_ref[0:1, :]).astype(F32)
    hot1 = (experts == ids_ref[1:2, :]).astype(F32)
    before = (
        lax.broadcasted_iota(jnp.int32, (tok, tok), 0)
        < lax.broadcasted_iota(jnp.int32, (tok, tok), 1)
    ).astype(F32).astype(BF)
    run0 = jnp.dot(hot0.astype(BF), before, preferred_element_type=F32)
    run1 = jnp.dot(hot1.astype(BF), before, preferred_element_type=F32)
    run1 = run1 + jnp.sum(hot0, axis=1, keepdims=True)
    base = experts.astype(F32) * float(cap)
    place0 = jnp.sum(hot0 * (run0 + base), axis=0, keepdims=True)
    place1 = jnp.sum(hot1 * (run1 + base), axis=0, keepdims=True)
    gate0, gate1 = gate_row_ref[0:1, :], gate_row_ref[1:2, :]
    tile = min(256, slots)

    @pl.loop(0, slots // tile)
    def _(i):
        here = pl.ds(pl.multiple_of(i * tile, tile), tile)
        slot = (lax.broadcasted_iota(jnp.int32, (tile, tok), 0) + i * tile).astype(F32)
        is0 = (slot == place0).astype(F32)
        is1 = (slot == place1).astype(F32)
        s0[here, :] = is0.astype(BF)
        s1[here, :] = is1.astype(BF)
        send_a[here, :] = (
            jnp.dot((is0 * gate0).astype(BF), hid_ref[:, :hid], preferred_element_type=F32)
            + jnp.dot((is1 * gate1).astype(BF), hid_ref[:, hid:], preferred_element_type=F32)
        ).astype(BF)

    pl.semaphore_wait(barrier, nj + 1 + jnp.where(crossed, 1, 0))

    swap = pltpu.make_async_remote_copy(
        src_ref=w_ref, dst_ref=w_full.at[shard(dp), :], send_sem=t_ss, recv_sem=t_rs,
        device_id=partner, device_id_type=MESH,
    )

    @pl.when(crossed)
    def _():
        swap.start()

    @pl.when(jnp.logical_not(crossed))
    def _():
        w_full[shard(z), :] = w_ref[...]

    def act_copy(i):
        t, device = peer(i)
        return pltpu.make_async_remote_copy(
            src_ref=send_a.at[chunk(t), :], dst_ref=recv_a.at[chunk(j), :],
            send_sem=a_ss, recv_sem=a_rs, device_id=device, device_id_type=MESH,
        )

    def grad_copy(i, b):
        t, device = peer(i)
        return pltpu.make_async_remote_copy(
            src_ref=send_g.at[b, chunk(t), :], dst_ref=recv_g.at[b, chunk(j), :],
            send_sem=g_ss.at[b], recv_sem=g_rs.at[b], device_id=device, device_id_type=MESH,
        )

    def reply_copy(i):
        t, device = peer(i)
        return pltpu.make_async_remote_copy(
            src_ref=reply.at[chunk(t), :], dst_ref=back.at[chunk(j), :],
            send_sem=p_ss, recv_sem=p_rs, device_id=device, device_id_type=MESH,
        )

    most = pl.ds(0, slots - cap)

    def wait_rows(ref, sem):
        pltpu.make_async_copy(ref, ref, sem).wait()

    @pl.loop(1, nj)
    def _(i):
        act_copy(i).start()

    recv_a[chunk(j), :] = send_a[chunk(j), :]

    for b in range(nb):

        @pl.loop(0, slots // tile)
        def _(i):
            here = pl.ds(pl.multiple_of(i * tile, tile), tile)
            send_g[b, here, :] = jnp.dot(
                s0[here, :] + s1[here, :], grads_ref[:, b * db : (b + 1) * db], preferred_element_type=F32
            ).astype(BF)

        @pl.loop(1, nj)
        def _(i):
            grad_copy(i, b).start()

        recv_g[b, chunk(j), :] = send_g[b, chunk(j), :]

    def ring_up(s):
        q = shard(lax.rem(z - s + 1 + nz, nz))
        return pltpu.make_async_remote_copy(
            src_ref=w_full.at[q, :], dst_ref=w_full.at[q, :], send_sem=gr_ss.at[s], recv_sem=gr_rs.at[s],
            device_id=up, device_id_type=MESH,
        )

    def ring_down(s):
        q = shard(lax.rem(z + s - 1, nz))
        return pltpu.make_async_remote_copy(
            src_ref=w_full.at[q, :], dst_ref=w_full.at[q, :], send_sem=gl_ss.at[s], recv_sem=gl_rs.at[s],
            device_id=down, device_id_type=MESH,
        )

    @pl.when(crossed)
    def _():
        swap.wait()

    ring_up(1).start()
    ring_down(1).start()

    @pl.loop(1, half)
    def _(s):
        ring_up(s).wait_recv()
        ring_up(s + 1).start()
        ring_down(s).wait_recv()

        @pl.when(s + 1 < half)
        def _():
            ring_down(s + 1).start()

    ring_up(half).wait_recv()

    def sum_up(s, b):
        return pltpu.make_async_remote_copy(
            src_ref=stage_r.at[b, s - 1], dst_ref=stage_r.at[b, s],
            send_sem=rr_ss.at[b, s], recv_sem=rr_rs.at[b, s], device_id=up, device_id_type=MESH,
        )

    def sum_down(s, b):
        return pltpu.make_async_remote_copy(
            src_ref=stage_l.at[b, s - 1], dst_ref=stage_l.at[b, s],
            send_sem=rl_ss.at[b, s], recv_sem=rl_rs.at[b, s], device_id=down, device_id_type=MESH,
        )

    def up_slice(s):
        return shard(lax.rem(z + half - s, nz))

    def down_slice(s):
        return shard(lax.rem(z - half - 1 + s + nz, nz))

    wait_rows(recv_a.at[most, :], a_rs)
    wide = min(256, hid)

    @pl.loop(0, hid // wide)
    def _(i):
        here = pl.ds(pl.multiple_of(i * wide, wide), wide)
        recv_at[here, :] = recv_a[:, here].T

    for b in range(nb):
        wait_rows(recv_g.at[b, most, :], g_rs.at[b])

        @pl.loop(0, hid // wide)
        def _(i):
            here = pl.ds(pl.multiple_of(i * wide, wide), wide)
            part[b, here, :] = jnp.dot(recv_at[here, :], recv_g[b], preferred_element_type=F32)

        stage_r[b, 0] = part[b, up_slice(1), :].astype(BF)
        stage_l[b, 0] = part[b, down_slice(1), :].astype(BF)
        sum_up(1, b).start()
        sum_down(1, b).start()

        @pl.loop(0, slots // tile)
        def _(i):
            here = pl.ds(pl.multiple_of(i * tile, tile), tile)
            product = lax.dot_general(
                recv_g[b, here, :], w_full[:, b * db : (b + 1) * db], (((1,), (1,)), ((), ())),
                preferred_element_type=F32,
            )
            if b == 0:
                racc[here, :] = product
            elif b < nb - 1:
                racc[here, :] += product
            else:
                reply[here, :] = (racc[here, :] + product).astype(BF)

    @pl.loop(1, nj)
    def _(i):
        reply_copy(i).start()

    back[chunk(j), :] = reply[chunk(j), :]

    @pl.loop(1, half)
    def _(s):
        @pl.loop(0, nb)
        def _(b):
            sum_up(s, b).wait_recv()

            @pl.when(s + 1 < half)
            def _():
                stage_r[b, s] = (stage_r[b, s].astype(F32) + part[b, up_slice(s + 1), :]).astype(BF)
                sum_up(s + 1, b).start()

            sum_down(s, b).wait_recv()
            stage_l[b, s] = (stage_l[b, s].astype(F32) + part[b, down_slice(s + 1), :]).astype(BF)
            sum_down(s + 1, b).start()

    def last_copy(b):
        return pltpu.make_async_remote_copy(
            src_ref=gfin.at[b], dst_ref=grecv.at[b], send_sem=f_ss.at[b], recv_sem=f_rs.at[b],
            device_id=partner, device_id_type=MESH,
        )

    @pl.loop(0, nb)
    def _(b):
        sum_down(half, b).wait_recv()
        total = part[b, shard(z), :] + stage_r[b, half - 1].astype(F32) + stage_l[b, half].astype(F32)
        gfin[b] = total.astype(BF)

        @pl.when(crossed)
        def _():
            last_copy(b).start()

        @pl.when(jnp.logical_not(crossed))
        def _():
            grecv[b] = total.astype(BF)

    wait_rows(back.at[most, :], p_rs)
    for k, picks in enumerate((s0, s1)):
        row = lax.dot_general(picks[...], back[...], (((0,), (0,)), ((), ())), preferred_element_type=F32)
        columns = slice(k * hid, (k + 1) * hid)
        dh_ref[:, columns] = (gate_col_ref[:, k : k + 1] * row).astype(BF)
        gg_ref[:, k : k + 1] = jnp.sum(hid_ref[:, columns].astype(F32) * row, axis=1, keepdims=True)

    fix_one = 1.0 - beta_one**STEP
    fix_two = 1.0 - beta_two**STEP
    for b in range(nb):

        @pl.when(crossed)
        def _():
            last_copy(b).wait()

        columns = slice(b * db, (b + 1) * db)
        gradient = grecv[b].astype(F32)
        moment = beta_one * m_ref[:, columns] + (1.0 - beta_one) * gradient
        second = beta_two * v_ref[:, columns] + (1.0 - beta_two) * gradient * gradient
        mo_ref[:, columns] = moment
        vo_ref[:, columns] = second
        up_ref[:, columns] = moment / fix_one / (jnp.sqrt(second / fix_two) + adam_eps)

    wait_rows(send_a.at[most, :], a_ss)
    wait_rows(reply.at[most, :], p_ss)
    for b in range(nb):
        wait_rows(send_g.at[b, most, :], g_ss.at[b])

    @pl.loop(1, half)
    def _(s):
        ring_up(s).wait_send()
        ring_down(s).wait_send()

        @pl.loop(0, nb)
        def _(b):
            sum_up(s, b).wait_send()
            sum_down(s, b).wait_send()

    ring_up(half).wait_send()

    @pl.loop(0, nb)
    def _(b):
        sum_down(half, b).wait_send()


def body(out_grad, hidden_act, expert_ids, gate_weight, down_weight, first_moment, second_moment):
    tok, top = expert_ids.shape
    width = out_grad.shape[1]
    hid = hidden_act.shape[2]
    nz = lax.axis_size("expert") // 2
    nj = 2 * lax.axis_size("dp")
    cap = 2 * tok * top // nj
    slots = nj * cap
    rows = hid // nz
    half = nz // 2
    nb = 4
    db = width // nb
    gate = gate_weight.astype(F32)
    dma = pltpu.SemaphoreType.DMA
    vmem = pl.BlockSpec(memory_space=pltpu.VMEM)
    dh, gg, mo, vo, up = pl.pallas_call(
        functools.partial(plane_kernel, (nz, nj, tok, cap, hid, nb, db)),
        out_shape=(
            jax.ShapeDtypeStruct((tok, top * hid), BF),
            jax.ShapeDtypeStruct((tok, top), F32),
            jax.ShapeDtypeStruct((rows, width), F32),
            jax.ShapeDtypeStruct((rows, width), F32),
            jax.ShapeDtypeStruct((rows, width), F32),
        ),
        in_specs=[vmem] * 8,
        out_specs=(vmem,) * 5,
        scratch_shapes=[
            pltpu.VMEM((slots, tok), BF),
            pltpu.VMEM((slots, tok), BF),
            pltpu.VMEM((slots, hid), BF),
            pltpu.VMEM((nb, slots, db), BF),
            pltpu.VMEM((slots, hid), BF),
            pltpu.VMEM((hid, slots), BF),
            pltpu.VMEM((nb, slots, db), BF),
            pltpu.VMEM((hid, width), BF),
            pltpu.VMEM((nb, hid, db), F32),
            pltpu.VMEM((slots, hid), F32),
            pltpu.VMEM((slots, hid), BF),
            pltpu.VMEM((slots, hid), BF),
            pltpu.VMEM((nb, half, rows, db), BF),
            pltpu.VMEM((nb, half + 1, rows, db), BF),
            pltpu.VMEM((nb, rows, db), BF),
            pltpu.VMEM((nb, rows, db), BF),
            dma, dma, dma((nb,)), dma((nb,)), dma, dma, dma, dma,
            dma((half + 1,)), dma((half + 1,)), dma((half + 1,)), dma((half + 1,)),
            dma((nb, half + 1)), dma((nb, half + 1)), dma((nb, half + 1)), dma((nb, half + 1)),
            dma((nb,)), dma((nb,)),
        ],
        compiler_params=pltpu.CompilerParams(
            collective_id=0, has_side_effects=True, vmem_limit_bytes=58 * 1024 * 1024
        ),
    )(
        out_grad, hidden_act.reshape(tok, top * hid), expert_ids.T, gate.T, gate,
        down_weight[0], first_moment[0], second_moment[0],
    )
    return dh.reshape(tok, top, hid), gg, mo[None], vo[None], up[None]


def solution(mesh):
    return jax.shard_map(
        body,
        mesh=mesh,
        in_specs=(
            P(("dp", "expert"), None),
            P(("dp", "expert"), None, None),
            P(("dp", "expert"), None),
            P(("dp", "expert"), None),
            P("expert", "dp", None),
            P("expert", "dp", None),
            P("expert", "dp", None),
        ),
        out_specs=(
            P(("dp", "expert"), None, None),
            P(("dp", "expert"), None),
            P("expert", "dp", None),
            P("expert", "dp", None),
            P("expert", "dp", None),
        ),
        check_vma=False,
    )
```

time: 444 us -> 198 us (0.45)
  the two profiles are of different devices: /device:TPU:6 before, /device:TPU:2 now
where the time goes in v1:
time: 198 us; the launch traced here: 197 us
  Pallas kernels  186 us (94%)
  local copies, waits for them, and re-layouts  10.3 us (5%)
    pallas_call x1, Pallas kernels, body(): pl.pallas_call(functools.partial(plane_kernel, (nz, nj, tok, cap, hid, nb...  186 us
    unnamed x16, local copies, waits for them, and re-layouts  6.6 us

profile of v1, /device:TPU:2, one launch (start us, length us, event | category | flops | bytes accessed | tf_op | source)
XLA Modules:
  0.0 197.4 jit_solution(4559331026744560544)
XLA Ops:
  0.6 0.0 copy-start.4
  0.6 0.7 copy-done.4
  1.3 0.1 copy.12
  1.5 0.7 fusion
  2.1 0.7 copy.13.gate_row_ref
  2.8 2.1 %copy.15 = bf16[32,8,2,768]{3,1,2,0:T(8,128)(2,1)} copy(bf16[32,8,2,768]{3,2,1,0:T(2,128)(2,1)} %bitcast.12) | data formatting | bytes 1572864
  4.9 185.8 %shard_map.110 = (bf16[256,1536]{1,0:T(8,128)(2,1)}, f32[256,2]{1,0:T(8,128)}, f32[48,2048]{1,0:T(8,128)}, f32[48,2048]{1,0:T(8,128)}, f32[48,2048]{1,0:T(8,128)}) custom-call(bf16[256,2048]{1,0:T(8,128)(2,1)} %grads_ref.1, bf16[256,1536]{1,0:T(8,128)(2,1)} %bitcast.11, s32[2,256]{1,0:T(2,128)} %bitcast.19, f32[2,256]{1,0:T(2,128)} %copy.13.gate_row_ref, ...), custom_call_target="tpu_custom_call" | custom-call | tf_op jit(solution)/shard_map/pallas_call | solution.py:342
  190.7 0.0 copy-start.3
  190.8 0.0 copy-start.2
  190.8 3.0 %reshape.17 = bf16[256,2,768]{2,1,0:T(2,128)(2,1)} reshape(bf16[256,1536]{1,0:T(8,128)(2,1)} %get-tuple-element.10) | data formatting | bytes 1572864 | tf_op jit(solution)/shard_map/reshape | solution.py:382
  193.8 0.0 copy-done.3
  193.8 0.7 copy.14
  194.4 0.0 copy-done.2
  194.4 0.0 copy-start.1
  194.4 0.7 copy.19
  195.2 0.4 copy-done.1
  195.6 0.0 copy-start
  195.6 0.7 copy.20
  196.3 0.4 copy-done
  196.7 0.7 copy.21
Async XLA Ops:
  0.6 0.7 copy-start.4
  190.7 3.0 %copy-start.3 = (f32[256,2]{1,0:T(8,128)S(1)}, f32[256,2]{1,0:T(8,128)}, u32[]{:S(2)}) copy-start(f32[256,2]{1,0:T(8,128)} %get-tuple-element.16) | copy-start | bytes 6148
  190.8 3.7 %copy-start.2 = (f32[48,2048]{1,0:T(8,128)S(1)}, f32[48,2048]{1,0:T(8,128)}, u32[]{:S(2)}) copy-start(f32[48,2048]{1,0:T(8,128)} %get-tuple-element.12) | copy-start | bytes 1179652
  194.4 1.1 copy-start.1
  195.6 1.1 copy-start

commit v2 on v1

v2 whole, which is shorter than its diff:
```python
import functools

import jax
import jax.numpy as jnp
from jax import lax
from jax.experimental import pallas as pl
from jax.experimental.pallas import tpu as pltpu
from jax.sharding import PartitionSpec as P

STEP = 11
MESH = pl.DeviceIdType.MESH
BF = jnp.bfloat16
F32 = jnp.float32

beta_one = 0.9
beta_two = 0.999
adam_eps = 1e-08


def plane_kernel(
    sizes, grads_ref, hid_ref, ids_ref, gate_ref, w_ref,
    dh_ref, gg_ref, grad_ref,
    pick, flat_pick, send_a, send_g, recv_a, recv_at, recv_g, w_full, part, reply, back,
    stage_r, stage_l, gfin, w_half, g_half,
    a_ss, a_rs, g_ss, g_rs, p_ss, p_rs, t_ss, t_rs, u_ss, u_rs, gr_ss, gr_rs, gl_ss, gl_rs,
    rr_ss, rr_rs, rl_ss, rl_rs, f_ss, f_rs, h_ss, h_rs,
):
    nz, nj, tok, cap, hid, nb, db, pieces = sizes
    half = nz // 2
    rows = hid // nz
    thin = rows // pieces
    slots = nj * cap
    own = 2 * tok
    dp = lax.axis_index("dp")
    ez = lax.axis_index("expert")
    z = ez // 2
    core = lax.rem(ez, 2)
    j = dp * 2 + core
    z_up, z_down = lax.rem(z + 1, nz), lax.rem(z + nz - 1, nz)
    up, down = (dp, z_up * 2 + core), (dp, z_down * 2 + core)

    def lag(k):
        return k * nz // pieces

    def mirrored(k):
        return lax.rem(dp + lag(k) - z + nz, nz)

    def entered(k, q):
        return lax.rem(dp + q - lag(k) + 2 * nz, nz)

    def peer(i):
        if nj != 32:
            t = lax.rem(j + i + 1, nj)
            return t, (t // 2, z * 2 + lax.rem(t, 2))
        turn = lax.rem(i, 4)
        cos = (1 - turn) * (1 - lax.rem(turn, 2))
        sin = (2 - turn) * lax.rem(turn, 2)
        reach = lax.rem(i // 4, 3)
        early = i < 24
        rest = 3 - turn
        dy = jnp.where(early, reach * cos + sin, 2 * (rest // 2))
        dx = jnp.where(early, cos - reach * sin, 2 * lax.rem(rest, 2))
        dc = jnp.where(early, 1 - i // 12, 1 - (i - 24) // 4)
        mirror = 1 - 2 * core
        y = lax.rem(dp // 4 + mirror * dy + 4, 4)
        x = lax.rem(lax.rem(dp, 4) + mirror * dx + 4, 4)
        c = lax.rem(core + dc, 2)
        return (y * 4 + x) * 2 + c, (y * 4 + x, z * 2 + c)

    def chunk(t):
        return pl.ds(pl.multiple_of(t * cap, cap), cap)

    def shard(q):
        return pl.ds(pl.multiple_of(q * rows, rows), rows)

    barrier = pltpu.get_barrier_semaphore()

    @pl.loop(0, nj - 1)
    def _(i):
        pl.semaphore_signal(barrier, inc=1, device_id=peer(i)[1], device_id_type=MESH)

    pl.semaphore_signal(barrier, inc=1, device_id=up, device_id_type=MESH)
    pl.semaphore_signal(barrier, inc=1, device_id=down, device_id_type=MESH)

    for k in range(pieces):

        @pl.when(mirrored(k) != z)
        def _():
            across = (dp, mirrored(k) * 2 + core)
            pl.semaphore_signal(barrier, inc=1, device_id=across, device_id_type=MESH)

    experts = lax.broadcasted_iota(jnp.int32, (nj, tok), 0)
    hot0 = (experts == ids_ref[0:1, :]).astype(F32)
    hot1 = (experts == ids_ref[1:2, :]).astype(F32)
    before = (
        lax.broadcasted_iota(jnp.int32, (tok, tok), 0)
        < lax.broadcasted_iota(jnp.int32, (tok, tok), 1)
    ).astype(F32).astype(BF)
    run0 = jnp.dot(hot0.astype(BF), before, preferred_element_type=F32)
    run1 = jnp.dot(hot1.astype(BF), before, preferred_element_type=F32)
    run1 = run1 + jnp.sum(hot0, axis=1, keepdims=True)
    rank0 = jnp.sum(hot0 * run0, axis=0, keepdims=True)
    rank1 = jnp.sum(hot1 * run1, axis=0, keepdims=True)
    place0 = ids_ref[0:1, :].astype(F32) * float(cap) + rank0
    place1 = ids_ref[1:2, :].astype(F32) * float(cap) + rank1
    blank = jnp.zeros((5, tok), F32)
    token = lax.broadcasted_iota(jnp.int32, (tok, own), 0) * 2
    slot = lax.broadcasted_iota(jnp.int32, (tok, own), 1)
    flat = jnp.zeros((8, own), F32)
    for k, rank in enumerate((rank0, rank1)):
        facts = jnp.concatenate(
            [ids_ref[k : k + 1, :].astype(F32), rank, gate_ref[k : k + 1, :].astype(F32), blank], axis=0
        )
        spread = (slot == token + k).astype(F32).astype(BF)
        flat = flat + jnp.dot(facts.astype(BF), spread, preferred_element_type=F32)
    place = flat[0:1, :] * float(cap) + flat[1:2, :]
    gate = flat[2:3, :]
    gate_col = flat.T[:, 2:3]
    tile = min(256, slots)

    pl.semaphore_wait(barrier, nj + 1 + sum(jnp.where(mirrored(k) != z, 1, 0) for k in range(pieces)))

    def piece(k):
        return pl.ds(pl.multiple_of(k * thin, thin), thin)

    def placed(p, k):
        return pl.ds(pl.multiple_of(p * rows + k * thin, thin), thin)

    def fold_copy(k):
        return pltpu.make_async_remote_copy(
            src_ref=w_ref.at[piece(k), :], dst_ref=w_half.at[k], send_sem=t_ss.at[k], recv_sem=t_rs.at[k],
            device_id=(dp, mirrored(k) * 2 + core), device_id_type=MESH,
        )

    def enter_copy(k):
        return pltpu.make_async_remote_copy(
            src_ref=w_half.at[k], dst_ref=w_full.at[placed(dp, k), :], send_sem=u_ss.at[k], recv_sem=u_rs.at[k],
            device_id=(mirrored(k), z * 2 + core), device_id_type=MESH,
        )

    @pl.loop(0, pieces)
    def _(k):
        @pl.when(mirrored(k) != z)
        def _():
            fold_copy(k).start()

        @pl.when(mirrored(k) == z)
        def _():
            w_half[k] = w_ref[piece(k), :]

    @pl.loop(0, slots // tile)
    def _(i):
        here = pl.ds(pl.multiple_of(i * tile, tile), tile)
        slot = (lax.broadcasted_iota(jnp.int32, (tile, tok), 0) + i * tile).astype(F32)
        pick[here, :] = ((slot == place0).astype(F32) + (slot == place1).astype(F32)).astype(BF)
        slot = (lax.broadcasted_iota(jnp.int32, (tile, own), 0) + i * tile).astype(F32)
        chosen = (slot == place).astype(F32)
        flat_pick[here, :] = chosen.astype(BF)
        send_a[here, :] = jnp.dot(
            (chosen * gate).astype(BF), hid_ref[...], preferred_element_type=F32
        ).astype(BF)

    def act_copy(i):
        t, device = peer(i)
        return pltpu.make_async_remote_copy(
            src_ref=send_a.at[chunk(t), :], dst_ref=recv_a.at[chunk(j), :],
            send_sem=a_ss, recv_sem=a_rs, device_id=device, device_id_type=MESH,
        )

    def grad_copy(i, b):
        t, device = peer(i)
        return pltpu.make_async_remote_copy(
            src_ref=send_g.at[b, chunk(t), :], dst_ref=recv_g.at[b, chunk(j), :],
            send_sem=g_ss.at[b], recv_sem=g_rs.at[b], device_id=device, device_id_type=MESH,
        )

    def reply_copy(i):
        t, device = peer(i)
        return pltpu.make_async_remote_copy(
            src_ref=reply.at[chunk(t), :], dst_ref=back.at[chunk(j), :],
            send_sem=p_ss, recv_sem=p_rs, device_id=device, device_id_type=MESH,
        )

    most = pl.ds(0, slots - cap)

    def wait_rows(ref, sem):
        pltpu.make_async_copy(ref, ref, sem).wait()

    @pl.loop(0, nj - 1)
    def _(i):
        act_copy(i).start()

    recv_a[chunk(j), :] = send_a[chunk(j), :]

    def send_block(b):
        @pl.loop(0, slots // tile)
        def _(i):
            here = pl.ds(pl.multiple_of(i * tile, tile), tile)
            send_g[b, here, :] = jnp.dot(
                pick[here, :], grads_ref[:, b * db : (b + 1) * db], preferred_element_type=F32
            ).astype(BF)

        @pl.loop(0, nj - 1)
        def _(i):
            grad_copy(i, b).start()

        recv_g[b, chunk(j), :] = send_g[b, chunk(j), :]

    def ring_up(s, k):
        q = placed(entered(k, lax.rem(z - s + 1 + nz, nz)), k)
        return pltpu.make_async_remote_copy(
            src_ref=w_full.at[q, :], dst_ref=w_full.at[q, :], send_sem=gr_ss.at[s, k], recv_sem=gr_rs.at[s, k],
            device_id=up, device_id_type=MESH,
        )

    def ring_down(s, k):
        q = placed(entered(k, lax.rem(z + s - 1, nz)), k)
        return pltpu.make_async_remote_copy(
            src_ref=w_full.at[q, :], dst_ref=w_full.at[q, :], send_sem=gl_ss.at[s, k], recv_sem=gl_rs.at[s, k],
            device_id=down, device_id_type=MESH,
        )

    def gather_enter():
        @pl.loop(0, pieces)
        def _(k):
            @pl.when(mirrored(k) != z)
            def _():
                fold_copy(k).wait()

            @pl.when(mirrored(k) != dp)
            def _():
                enter_copy(k).start()

            @pl.when(mirrored(k) == dp)
            def _():
                w_full[placed(dp, k), :] = w_half[k]

    def gather_begin():
        @pl.loop(0, pieces)
        def _(k):
            @pl.when(mirrored(k) != dp)
            def _():
                enter_copy(k).wait()

            ring_up(1, k).start()
            if half > 1:
                ring_down(1, k).start()

    def gather_steps(first, last):
        @pl.loop(first, min(last, half - 1) + 1)
        def _(s):
            @pl.loop(0, pieces)
            def _(k):
                ring_up(s, k).wait_recv()
                ring_up(s + 1, k).start()
                ring_down(s, k).wait_recv()

                @pl.when(s + 1 < half)
                def _():
                    ring_down(s + 1, k).start()

        if last >= half:

            @pl.loop(0, pieces)
            def _(k):
                ring_up(half, k).wait_recv()

    def sum_up(s, b):
        return pltpu.make_async_remote_copy(
            src_ref=stage_r.at[b, s - 1], dst_ref=stage_r.at[b, s],
            send_sem=rr_ss.at[b, s], recv_sem=rr_rs.at[b, s], device_id=up, device_id_type=MESH,
        )

    def sum_down(s, b):
        return pltpu.make_async_remote_copy(
            src_ref=stage_l.at[b, s - 1], dst_ref=stage_l.at[b, s],
            send_sem=rl_ss.at[b, s], recv_sem=rl_rs.at[b, s], device_id=down, device_id_type=MESH,
        )

    def up_slice(s):
        return shard(lax.rem(z + half - s, nz))

    def down_slice(s):
        return shard(lax.rem(z - half - 1 + s + nz, nz))

    def leave_copy(b, k):
        return pltpu.make_async_remote_copy(
            src_ref=gfin.at[b, piece(k), :], dst_ref=g_half.at[b, k], send_sem=f_ss.at[b, k], recv_sem=f_rs.at[b, k],
            device_id=(entered(k, z), z * 2 + core), device_id_type=MESH,
        )

    def home_copy(b, k):
        return pltpu.make_async_remote_copy(
            src_ref=g_half.at[b, k], dst_ref=grad_ref.at[piece(k), b * db : (b + 1) * db],
            send_sem=h_ss.at[b, k], recv_sem=h_rs.at[b, k],
            device_id=(dp, mirrored(k) * 2 + core), device_id_type=MESH,
        )

    def home(b):
        @pl.loop(0, pieces)
        def _(k):
            @pl.when(entered(k, z) != dp)
            def _():
                leave_copy(b, k).wait()

            @pl.when(mirrored(k) != z)
            def _():
                home_copy(b, k).start()

            @pl.when(mirrored(k) == z)
            def _():
                grad_ref[piece(k), b * db : (b + 1) * db] = g_half[b, k]

    following = {}

    def sum_begin(b):
        stage_l[b, 0] = part[b, down_slice(1), :].astype(BF)
        sum_down(1, b).start()
        if half > 1:
            stage_r[b, 0] = part[b, up_slice(1), :].astype(BF)
            sum_up(1, b).start()
        following[b] = 1

    def sum_end(b):
        sum_down(half, b).wait_recv()
        total = part[b, shard(z), :] + stage_r[b, half - 1].astype(F32) + stage_l[b, half].astype(F32)
        gfin[b] = total.astype(BF)

        @pl.loop(0, pieces)
        def _(k):
            @pl.when(entered(k, z) != dp)
            def _():
                leave_copy(b, k).start()

            @pl.when(entered(k, z) == dp)
            def _():
                g_half[b, k] = gfin[b, piece(k), :]

        if b > 0:
            home(b - 1)

    def sum_steps(count):
        while count and following:
            n = min([count] + [half - s for s in following.values()])

            @pl.loop(0, n)
            def _(i):
                for b, first in following.items():
                    s = first + i
                    sum_down(s, b).wait_recv()
                    stage_l[b, s] = (stage_l[b, s].astype(F32) + part[b, down_slice(s + 1), :]).astype(BF)
                    sum_down(s + 1, b).start()
                    sum_up(s, b).wait_recv()

                    @pl.when(s + 1 < half)
                    def _():
                        stage_r[b, s] = (stage_r[b, s].astype(F32) + part[b, up_slice(s + 1), :]).astype(BF)
                        sum_up(s + 1, b).start()

            for b in list(following):
                following[b] += n
                if following[b] == half:
                    del following[b]
                    sum_end(b)
            count -= n

    wide = min(256, hid)

    def turn_acts():
        wait_rows(recv_a.at[most, :], a_rs)

        @pl.loop(0, hid // wide)
        def _(i):
            here = pl.ds(pl.multiple_of(i * wide, wide), wide)
            turned = recv_a[:, here].T
            for u in range(wide // thin):
                block = i * (wide // thin) + u
                k = lax.rem(block, pieces)
                q = lax.rem(block // pieces - dp + lag(k) + nz, nz)
                recv_at[placed(q, k), :] = turned[u * thin : (u + 1) * thin, :]

    def sum_block(b):
        wait_rows(recv_g.at[b, most, :], g_rs.at[b])

        @pl.loop(0, hid // wide)
        def _(i):
            here = pl.ds(pl.multiple_of(i * wide, wide), wide)
            part[b, here, :] = jnp.dot(recv_at[here, :], recv_g[b], preferred_element_type=F32)

        sum_begin(b)

    def reply_rows(i):
        here = slice(i * tile, (i + 1) * tile)
        reply[here, :] = sum(
            lax.dot_general(
                recv_g[b, here, :], w_full[:, b * db : (b + 1) * db], (((1,), (1,)), ((), ())),
                preferred_element_type=F32,
            )
            for b in range(nb)
        ).astype(BF)

    def gather_step(s):
        if s <= half:
            gather_steps(s, s)

    send_block(0)
    gather_enter()
    send_block(1)
    gather_begin()
    send_block(2)
    gather_step(1)
    send_block(3)
    gather_step(2)
    gather_step(3)
    turn_acts()
    sum_block(0)
    gather_step(4)
    sum_steps(1)
    gather_step(5)
    sum_steps(1)
    sum_block(1)
    gather_step(6)
    sum_steps(1)
    gather_step(7)
    sum_steps(1)
    sum_block(2)
    gather_step(8)
    sum_steps(2)
    sum_block(3)
    for i in range(slots // tile):
        reply_rows(i)
        sum_steps(1)

    @pl.loop(0, nj - 1)
    def _(i):
        reply_copy(i).start()

    back[chunk(j), :] = reply[chunk(j), :]
    sum_steps(half * nb)
    home(nb - 1)

    wait_rows(back.at[most, :], p_rs)
    row = lax.dot_general(flat_pick[...], back[...], (((0,), (0,)), ((), ())), preferred_element_type=F32)
    dh_ref[...] = (gate_col * row).astype(BF)
    sums = jnp.sum(hid_ref[...].astype(F32) * row, axis=1, keepdims=True)
    token = lax.broadcasted_iota(jnp.int32, (own, tok), 1) * 2
    slot = lax.broadcasted_iota(jnp.int32, (own, tok), 0)
    for k in range(2):
        gg_ref[k : k + 1, :] = jnp.sum(jnp.where(slot == token + k, sums, 0.0), axis=0, keepdims=True)

    wait_rows(send_a.at[most, :], a_ss)
    wait_rows(reply.at[most, :], p_ss)
    for b in range(nb):
        wait_rows(send_g.at[b, most, :], g_ss.at[b])

    @pl.loop(1, half)
    def _(s):
        @pl.loop(0, pieces)
        def _(k):
            ring_up(s, k).wait_send()
            ring_down(s, k).wait_send()

        @pl.loop(0, nb)
        def _(b):
            sum_up(s, b).wait_send()
            sum_down(s, b).wait_send()

    @pl.loop(0, pieces)
    def _(k):
        ring_up(half, k).wait_send()

    @pl.loop(0, nb)
    def _(b):
        sum_down(half, b).wait_send()

    for b in range(nb):

        @pl.loop(0, pieces)
        def _(k):
            @pl.when(mirrored(k) != z)
            def _():
                home_copy(b, k).wait()


def body(out_grad, hidden_act, expert_ids, gate_weight, down_weight, first_moment, second_moment):
    tok, top = expert_ids.shape
    width = out_grad.shape[1]
    hid = hidden_act.shape[2]
    nz = lax.axis_size("expert") // 2
    nj = 2 * lax.axis_size("dp")
    cap = 2 * tok * top // nj
    slots = nj * cap
    own = tok * top
    rows = hid // nz
    half = nz // 2
    nb = 4
    db = width // nb
    pieces = rows // 16
    dma = pltpu.SemaphoreType.DMA
    vmem = pl.BlockSpec(memory_space=pltpu.VMEM)
    dh, gg, gradient = pl.pallas_call(
        functools.partial(plane_kernel, (nz, nj, tok, cap, hid, nb, db, pieces)),
        out_shape=(
            jax.ShapeDtypeStruct((own, hid), BF),
            jax.ShapeDtypeStruct((top, tok), F32),
            jax.ShapeDtypeStruct((rows, width), BF),
        ),
        in_specs=[vmem] * 5,
        out_specs=(vmem,) * 3,
        scratch_shapes=[
            pltpu.VMEM((slots, tok), BF),
            pltpu.VMEM((slots, own), BF),
            pltpu.VMEM((slots, hid), BF),
            pltpu.VMEM((nb, slots, db), BF),
            pltpu.VMEM((slots, hid), BF),
            pltpu.VMEM((hid, slots), BF),
            pltpu.VMEM((nb, slots, db), BF),
            pltpu.VMEM((hid, width), BF),
            pltpu.VMEM((nb, hid, db), F32),
            pltpu.VMEM((slots, hid), BF),
            pltpu.VMEM((slots, hid), BF),
            pltpu.VMEM((nb, half, rows, db), BF),
            pltpu.VMEM((nb, half + 1, rows, db), BF),
            pltpu.VMEM((nb, rows, db), BF),
            pltpu.VMEM((pieces, rows // pieces, width), BF),
            pltpu.VMEM((nb, pieces, rows // pieces, db), BF),
            dma, dma, dma((nb,)), dma((nb,)), dma, dma,
            dma((pieces,)), dma((pieces,)), dma((pieces,)), dma((pieces,)),
            dma((half + 1, pieces)), dma((half + 1, pieces)), dma((half + 1, pieces)), dma((half + 1, pieces)),
            dma((nb, half + 1)), dma((nb, half + 1)), dma((nb, half + 1)), dma((nb, half + 1)),
            dma((nb, pieces)), dma((nb, pieces)), dma((nb, pieces)), dma((nb, pieces)),
        ],
        compiler_params=pltpu.CompilerParams(
            collective_id=0, has_side_effects=True, vmem_limit_bytes=58 * 1024 * 1024
        ),
    )(
        out_grad, hidden_act.reshape(own, hid), expert_ids.T, gate_weight.T, down_weight[0],
    )
    gradient = gradient.astype(F32)
    moment_new = beta_one * first_moment[0] + (1.0 - beta_one) * gradient
    second_new = beta_two * second_moment[0] + (1.0 - beta_two) * gradient * gradient
    fix_one = 1.0 - beta_one**STEP
    fix_two = 1.0 - beta_two**STEP
    update = moment_new / fix_one / (jnp.sqrt(second_new / fix_two) + adam_eps)
    return dh.reshape(tok, top, hid), gg.T, moment_new[None], second_new[None], update[None]


def solution(mesh):
    return jax.shard_map(
        body,
        mesh=mesh,
        in_specs=(
            P(("dp", "expert"), None),
            P(("dp", "expert"), None, None),
            P(("dp", "expert"), None),
            P(("dp", "expert"), None),
            P("expert", "dp", None),
            P("expert", "dp", None),
            P("expert", "dp", None),
        ),
        out_specs=(
            P(("dp", "expert"), None, None),
            P(("dp", "expert"), None),
            P("expert", "dp", None),
            P("expert", "dp", None),
            P("expert", "dp", None),
        ),
        check_vma=False,
    )
```

time: 198 us -> 165 us (0.83)
  the two profiles are of different devices: /device:TPU:2 before, /device:TPU:6 now
where the time goes in v2:
time: 165 us; the launch traced here: 164 us
  Pallas kernels  155 us (94%)
  local copies, waits for them, and re-layouts  7.14 us (4%)
    pallas_call x1, Pallas kernels, body(): pl.pallas_call(functools.partial(plane_kernel, (nz, nj, tok, cap, hid, nb...  155 us

profile of v2, /device:TPU:6, one launch (start us, length us, event | category | flops | bytes accessed | tf_op | source)
XLA Modules:
  0.0 164.4 jit_solution(16624077665898388936)
XLA Ops:
  0.6 3.0 %reshape.20.hid_ref = bf16[512,768]{1,0:T(8,128)(2,1)} reshape(bf16[256,2,768]{2,1,0:T(2,128)(2,1)} %param.8) | data formatting | bytes 1572864 | tf_op jit(solution)/shard_map/reshape | solution.py:537
  3.6 155.5 %shard_map.110 = (bf16[512,768]{1,0:T(8,128)(2,1)}, f32[2,256]{1,0:T(2,128)}, bf16[48,2048]{1,0:T(8,128)(2,1)}) custom-call(bf16[256,2048]{1,0:T(8,128)(2,1)} %grads_ref.1, bf16[512,768]{1,0:T(8,128)(2,1)} %reshape.20.hid_ref, s32[2,256]{1,0:T(2,128)} %bitcast.24, bf16[2,256]{1,0:T(2,128)(2,1)} %bitcast.25, bf16[48,2048]{1,0:T(8,128)(2,1)} %bitcast.22), custom_call_target="tpu_custom_call" | custom-call | tf_op jit(solution)/shard_map/pallas_call | solution.py:501
  159.1 0.0 copy-start
  159.1 0.0 copy-start.1
  159.1 0.0 copy-start.2
  159.1 2.9 %reshape.21 = bf16[256,2,768]{2,1,0:T(2,128)(2,1)} reshape(bf16[512,768]{1,0:T(8,128)(2,1)} %get-tuple-element.8) | data formatting | bytes 1572864 | tf_op jit(solution)/shard_map/reshape | solution.py:545
  162.0 0.0 copy-done
  162.0 0.0 copy-done.1
  162.0 0.0 copy-done.2
  162.0 1.1 divide_bitcast_fusion
  163.2 0.0 copy-start.3
  163.2 0.7 copy-done.3
  163.8 0.6 copy.13
Async XLA Ops:
  159.1 3.0 %copy-start = (f32[1,48,2048]{2,1,0:T(8,128)S(1)}, f32[1,48,2048]{2,1,0:T(8,128)}, u32[]{:S(2)}) copy-start(f32[1,48,2048]{2,1,0:T(8,128)} %param.12) | copy-start | bytes 1179652
  159.1 3.0 %copy-start.1 = (f32[1,48,2048]{2,1,0:T(8,128)S(1)}, f32[1,48,2048]{2,1,0:T(8,128)}, u32[]{:S(2)}) copy-start(f32[1,48,2048]{2,1,0:T(8,128)} %param.13) | copy-start | bytes 1179652
  159.1 2.9 %copy-start.2 = (bf16[48,2048]{1,0:T(8,128)(2,1)S(1)}, bf16[48,2048]{1,0:T(8,128)(2,1)}, u32[]{:S(2)}) copy-start(bf16[48,2048]{1,0:T(8,128)(2,1)} %get-tuple-element.10) | copy-start | bytes 589828
  163.2 0.7 copy-start.3

commit v3 on v2

--- a/solution.py
+++ b/solution.py
@@ -413,19 +413,15 @@
     gather_step(2)
     gather_step(3)
     turn_acts()
+    gather_step(4)
+    gather_step(5)
+    gather_step(6)
     sum_block(0)
-    gather_step(4)
+    gather_step(7)
+    gather_step(8)
+    sum_block(1)
+    sum_block(2)
     sum_steps(1)
-    gather_step(5)
-    sum_steps(1)
-    sum_block(1)
-    gather_step(6)
-    sum_steps(1)
-    gather_step(7)
-    sum_steps(1)
-    sum_block(2)
-    gather_step(8)
-    sum_steps(2)
     sum_block(3)
     for i in range(slots // tile):
         reply_rows(i)

time: 165 us -> 164 us (level)
  the two profiles are of different devices: /device:TPU:6 before, /device:TPU:24 now
where the time goes in v3:
time: 164 us; the launch traced here: 163 us
  Pallas kernels  154 us (94%)
  local copies, waits for them, and re-layouts  7.14 us (4%)
    pallas_call x1, Pallas kernels, body(): pl.pallas_call(functools.partial(plane_kernel, (nz, nj, tok, cap, hid, nb...  154 us

profile of v3, /device:TPU:24, one launch (start us, length us, event | category | flops | bytes accessed | tf_op | source)
XLA Modules:
  0.0 163.4 jit_solution(3357966328971565829)
XLA Ops:
  0.6 3.0 %reshape.20.hid_ref = bf16[512,768]{1,0:T(8,128)(2,1)} reshape(bf16[256,2,768]{2,1,0:T(2,128)(2,1)} %param.8) | data formatting | bytes 1572864 | tf_op jit(solution)/shard_map/reshape | solution.py:533
  3.6 154.5 %shard_map.110 = (bf16[512,768]{1,0:T(8,128)(2,1)}, f32[2,256]{1,0:T(2,128)}, bf16[48,2048]{1,0:T(8,128)(2,1)}) custom-call(bf16[256,2048]{1,0:T(8,128)(2,1)} %grads_ref.1, bf16[512,768]{1,0:T(8,128)(2,1)} %reshape.20.hid_ref, s32[2,256]{1,0:T(2,128)} %bitcast.24, bf16[2,256]{1,0:T(2,128)(2,1)} %bitcast.25, bf16[48,2048]{1,0:T(8,128)(2,1)} %bitcast.22), custom_call_target="tpu_custom_call" | custom-call | tf_op jit(solution)/shard_map/pallas_call | solution.py:497
  158.1 0.0 copy-start
  158.1 0.0 copy-start.1
  158.1 0.0 copy-start.2
  158.1 2.9 %reshape.21 = bf16[256,2,768]{2,1,0:T(2,128)(2,1)} reshape(bf16[512,768]{1,0:T(8,128)(2,1)} %get-tuple-element.8) | data formatting | bytes 1572864 | tf_op jit(solution)/shard_map/reshape | solution.py:541
  161.0 0.0 copy-done
  161.0 0.0 copy-done.1
  161.0 0.0 copy-done.2
  161.0 1.1 divide_bitcast_fusion
  162.2 0.0 copy-start.3
  162.2 0.7 copy-done.3
  162.8 0.6 copy.13
Async XLA Ops:
  158.1 3.0 %copy-start = (f32[1,48,2048]{2,1,0:T(8,128)S(1)}, f32[1,48,2048]{2,1,0:T(8,128)}, u32[]{:S(2)}) copy-start(f32[1,48,2048]{2,1,0:T(8,128)} %param.12) | copy-start | bytes 1179652
  158.1 3.0 %copy-start.1 = (f32[1,48,2048]{2,1,0:T(8,128)S(1)}, f32[1,48,2048]{2,1,0:T(8,128)}, u32[]{:S(2)}) copy-start(f32[1,48,2048]{2,1,0:T(8,128)} %param.13) | copy-start | bytes 1179652
  158.1 2.9 %copy-start.2 = (bf16[48,2048]{1,0:T(8,128)(2,1)S(1)}, bf16[48,2048]{1,0:T(8,128)(2,1)}, u32[]{:S(2)}) copy-start(bf16[48,2048]{1,0:T(8,128)(2,1)} %get-tuple-element.10) | copy-start | bytes 589828
  162.2 0.7 copy-start.3

commit v4 on v3

--- a/solution.py
+++ b/solution.py
@@ -311,7 +311,7 @@
             def _():
                 grad_ref[piece(k), b * db : (b + 1) * db] = g_half[b, k]
 
-    following = {}
+    following, leaving = {}, []
 
     def sum_begin(b):
         stage_l[b, 0] = part[b, down_slice(1), :].astype(BF)
@@ -335,9 +335,6 @@
             @pl.when(entered(k, z) == dp)
             def _():
                 g_half[b, k] = gfin[b, piece(k), :]
-
-        if b > 0:
-            home(b - 1)
 
     def sum_steps(count):
         while count and following:
@@ -357,11 +354,14 @@
                         stage_r[b, s] = (stage_r[b, s].astype(F32) + part[b, up_slice(s + 1), :]).astype(BF)
                         sum_up(s + 1, b).start()
 
+            while leaving:
+                home(leaving.pop(0))
             for b in list(following):
                 following[b] += n
                 if following[b] == half:
                     del following[b]
                     sum_end(b)
+                    leaving.append(b)
             count -= n
 
     wide = min(256, hid)
@@ -433,11 +433,12 @@
 
     back[chunk(j), :] = reply[chunk(j), :]
     sum_steps(half * nb)
-    home(nb - 1)
 
     wait_rows(back.at[most, :], p_rs)
     row = lax.dot_general(flat_pick[...], back[...], (((0,), (0,)), ((), ())), preferred_element_type=F32)
     dh_ref[...] = (gate_col * row).astype(BF)
+    while leaving:
+        home(leaving.pop(0))
     sums = jnp.sum(hid_ref[...].astype(F32) * row, axis=1, keepdims=True)
     token = lax.broadcasted_iota(jnp.int32, (own, tok), 1) * 2
     slot = lax.broadcasted_iota(jnp.int32, (own, tok), 0)

time: 164 us -> 161 us (0.982)
  the two profiles are of different devices: /device:TPU:24 before, /device:TPU:6 now
where the time goes in v4:
time: 161 us; the launch traced here: 159 us
  Pallas kernels  150 us (93%)
  local copies, waits for them, and re-layouts  7.14 us (4%)
    pallas_call x1, Pallas kernels, body(): pl.pallas_call(functools.partial(plane_kernel, (nz, nj, tok, cap, hid, nb...  150 us

profile of v4, /device:TPU:6, one launch (start us, length us, event | category | flops | bytes accessed | tf_op | source)
XLA Modules:
  0.0 159.4 jit_solution(17393916232362358888)
XLA Ops:
  0.6 3.0 %reshape.20.hid_ref = bf16[512,768]{1,0:T(8,128)(2,1)} reshape(bf16[256,2,768]{2,1,0:T(2,128)(2,1)} %param.8) | data formatting | bytes 1572864 | tf_op jit(solution)/shard_map/reshape | solution.py:534
  3.6 150.5 %shard_map.110 = (bf16[512,768]{1,0:T(8,128)(2,1)}, f32[2,256]{1,0:T(2,128)}, bf16[48,2048]{1,0:T(8,128)(2,1)}) custom-call(bf16[256,2048]{1,0:T(8,128)(2,1)} %grads_ref.1, bf16[512,768]{1,0:T(8,128)(2,1)} %reshape.20.hid_ref, s32[2,256]{1,0:T(2,128)} %bitcast.24, bf16[2,256]{1,0:T(2,128)(2,1)} %bitcast.25, bf16[48,2048]{1,0:T(8,128)(2,1)} %bitcast.22), custom_call_target="tpu_custom_call" | custom-call | tf_op jit(solution)/shard_map/pallas_call | solution.py:498
  154.1 0.0 copy-start
  154.1 0.0 copy-start.1
  154.1 0.0 copy-start.2
  154.1 2.9 %reshape.21 = bf16[256,2,768]{2,1,0:T(2,128)(2,1)} reshape(bf16[512,768]{1,0:T(8,128)(2,1)} %get-tuple-element.8) | data formatting | bytes 1572864 | tf_op jit(solution)/shard_map/reshape | solution.py:542
  157.0 0.0 copy-done
  157.0 0.0 copy-done.1
  157.0 0.0 copy-done.2
  157.1 1.1 divide_bitcast_fusion
  158.2 0.0 copy-start.3
  158.2 0.7 copy-done.3
  158.9 0.6 copy.13
Async XLA Ops:
  154.1 3.0 %copy-start = (f32[1,48,2048]{2,1,0:T(8,128)S(1)}, f32[1,48,2048]{2,1,0:T(8,128)}, u32[]{:S(2)}) copy-start(f32[1,48,2048]{2,1,0:T(8,128)} %param.12) | copy-start | bytes 1179652
  154.1 3.0 %copy-start.1 = (f32[1,48,2048]{2,1,0:T(8,128)S(1)}, f32[1,48,2048]{2,1,0:T(8,128)}, u32[]{:S(2)}) copy-start(f32[1,48,2048]{2,1,0:T(8,128)} %param.13) | copy-start | bytes 1179652
  154.1 2.9 %copy-start.2 = (bf16[48,2048]{1,0:T(8,128)(2,1)S(1)}, bf16[48,2048]{1,0:T(8,128)(2,1)}, u32[]{:S(2)}) copy-start(bf16[48,2048]{1,0:T(8,128)(2,1)} %get-tuple-element.10) | copy-start | bytes 589828
  158.2 0.7 copy-start.3
